TPU v7x, 32 devices: a whole 2x2x4 slice. The times are simulated.
32 devices in a mesh: row: 8 (over z, y), col: 4 (over x, core).
Axes of the slice: x: 2, y: 2, z: 4, core: 2. Of those that a mesh axis runs over, the one named last changes fastest.
Arguments:
- density: float32 [8, 8, 4, 128, 128], P('row', 'col'), as said below
- pattern: int32 [8, 8, 4], P('row', 'col'), may hold values from 0 to 8, as said below
- retained: int32 [8, 8, 4], P('row', 'col'), may hold values from 0 to 8, as said below
Outputs:
- purified: float32 [8, 8, 4, 128, 128], P('row', 'col')
Inputs may be any that keep to these rules, and one draw needn't show every extreme that they name: Slot 0 of every block row holds code 4, the site itself; the 4 codes of a block row are distinct; the pattern is symmetric: x holds c exactly when x + offset(c) holds 8 - c. `retained`: slot 0 of every block row holds code 4, the site itself; the 4 codes of a block row are distinct; the pattern is symmetric: x holds c exactly when x + offset(c) holds 8 - c. `density`: the matrix is symmetric: the block of x on code c is the transpose of the block of x + offset(c) on code 8 - c, and every block on code 4 is symmetric.
All inputs are finite; a program needn't handle non-finite values.
Results may differ from a plain program's by a relative error of at most 0.0003.
Values sent between devices are 32-bit elements; how exact they have to be, the bound alone decides.
A program may use at most 64 MiB of HBM per device.

v0:
```python
import jax
import jax.numpy as jnp
from jax import lax
from jax.sharding import PartitionSpec as P


def extended(x, sides, width):
    for axis, dim in sides:
        count, length = (lax.axis_size(axis), x.shape[dim])
        up = [(i, (i + 1) % count) for i in range(count)]
        down = [(j, i) for i, j in up]
        last = lax.slice_in_dim(x, length - width, length, axis=dim)
        initial = lax.slice_in_dim(x, 0, width, axis=dim)
        before = lax.ppermute(last, axis, up)
        after = lax.ppermute(initial, axis, down)
        x = jnp.concatenate([before, x, after], axis=dim)
    return x


def offsets(codes):
    return (codes // 3 - 1, codes % 3 - 1)


def local_product(left_blocks, left_codes, right_blocks, right_codes, out_codes):
    lattice_a = left_codes.shape[0]
    lattice_b = left_codes.shape[1]
    slot_count = left_codes.shape[2]
    width_b = right_blocks.shape[1]
    flat_right = right_blocks.reshape((-1,) + right_blocks.shape[2:])
    flat_codes = right_codes.reshape((-1, slot_count))
    flat_left = left_blocks.reshape((-1,) + left_blocks.shape[2:])
    grid_a = jnp.arange(lattice_a, dtype=jnp.int32)[:, None]
    grid_b = jnp.arange(lattice_b, dtype=jnp.int32)[None, :]
    out_a, out_b = offsets(out_codes.reshape((-1, slot_count)))
    summed = jnp.zeros(flat_left.shape, jnp.float32)
    for slot_idx in range(slot_count):
        step_a, step_b = offsets(left_codes[:, :, slot_idx])
        target = ((grid_a + 1 + step_a) * width_b + grid_b + 1 + step_b).reshape(-1)
        near_blocks = jnp.take(flat_right, target, axis=0)
        their_a, their_b = offsets(jnp.take(flat_codes, target, axis=0))
        reach_a = step_a.reshape(-1)[:, None] + their_a
        reach_b = step_b.reshape(-1)[:, None] + their_b
        matches = (
            (reach_a[:, :, None] == out_a[:, None, :]) & (reach_b[:, :, None] == out_b[:, None, :])
        ).astype(jnp.float32)
        products = jnp.einsum(
            "xij,xtjk->xtik", flat_left[:, slot_idx], near_blocks, precision=lax.Precision.HIGHEST
        )
        summed = summed + jnp.einsum(
            "xtu,xtik->xuik", matches, products, precision=lax.Precision.HIGHEST
        )
    return summed.reshape(left_blocks.shape)


def widen(blocks, codes):
    return (
        extended(blocks, (("row", 0), ("col", 1)), 1),
        extended(codes, (("row", 0), ("col", 1)), 1),
    )


def purify_step(iterate, codes, retained, near_blocks, near_codes):
    square = local_product(iterate, codes, near_blocks, near_codes, retained)
    cubed = local_product(square, retained, near_blocks, near_codes, retained)
    return 3.0 * square - 2.0 * cubed


def on_device(density, pattern, retained):
    near_blocks, near_codes = widen(density, pattern)
    iterate = purify_step(density, pattern, retained, near_blocks, near_codes)
    near_blocks, near_codes = widen(iterate, retained)
    return purify_step(iterate, retained, retained, near_blocks, near_codes)


def solution(mesh):
    return jax.shard_map(
        on_device,
        mesh=mesh,
        in_specs=(P("row", "col", None, None, None), P("row", "col", None), P("row", "col", None)),
        out_specs=P("row", "col", None, None, None),
        check_vma=False,
    )
```

profile of v0, /device:TPU:1, one launch (start us, length us, event | category | flops | bytes accessed | tf_op | source)
XLA Modules:
  0.0 177.2 jit_solution(541721025465466117)
XLA Ops:
  0.0 2.1 %collective-permute-start.8 = (f32[1,2,4,128,128]{4,3,2,1,0:T(8,128)}, f32[1,2,4,128,128]{4,3,2,1,0:T(8,128)S(1)}, u32[]{:S(2)}, u32[]{:S(2)}) collective-permute-start(f32[1,2,4,128,128]{4,3,2,1,0:T(8,128)} %param.7), channel_id=1, source_target_pairs={{0,4},{4,8},{8,12},{12,16},{16,20},{20,24},{24,28},{28,0},{1,5},{5... | collective-permute-start | bytes 1572872 | tf_op jit(solution)/shard_map/ppermute | solution.py:14
  2.1 3.0 %collective-permute-start.9 = (f32[1,2,4,128,128]{4,3,2,1,0:T(8,128)}, f32[1,2,4,128,128]{4,3,2,1,0:T(8,128)S(1)}, u32[]{:S(2)}, u32[]{:S(2)}) collective-permute-start(f32[1,2,4,128,128]{4,3,2,1,0:T(8,128)} %param.7), channel_id=1, source_target_pairs={{4,0},{8,4},{12,8},{16,12},{20,16},{24,20},{28,24},{0,28},{5,1},{9... | collective-permute-start | bytes 1572872 | tf_op jit(solution)/shard_map/ppermute | solution.py:15
  5.1 4.2 %collective-permute-start.5 = (s32[1,2,4]{2,1,0:T(2,128)}, s32[1,2,4]{2,1,0:T(2,128)S(1)}, u32[]{:S(2)}, u32[]{:S(2)}) collective-permute-start(s32[1,2,4]{2,1,0:T(2,128)} %param.8), channel_id=1, source_target_pairs={{4,0},{8,4},{12,8},{16,12},{20,16},{24,20},{28,24},{0,28},{5,1},{9... | collective-permute-start | bytes 104 | tf_op jit(solution)/shard_map/ppermute | solution.py:15
  14.7 9.5 %collective-permute-done.4 = s32[1,2,4]{2,1,0:T(2,128)S(1)} collective-permute-done((s32[1,2,4]{2,1,0:T(2,128)}, s32[1,2,4]{2,1,0:T(2,128)S(1)}, u32[]{:S(2)}, u32[]{:S(2)}) %collective-permute-start.4) | collective-permute-done | bytes 64 | tf_op jit(solution)/shard_map/ppermute | solution.py:14
  24.2 5.1 %collective-permute-start.1 = (s32[1,2,4]{2,1,0:T(2,128)}, s32[1,2,4]{2,1,0:T(2,128)S(1)}, u32[]{:S(2)}, u32[]{:S(2)}) collective-permute-start(s32[1,2,4]{2,1,0:T(2,128)} %param.9), channel_id=1, source_target_pairs={{4,0},{8,4},{12,8},{16,12},{20,16},{24,20},{28,24},{0,28},{5,1},{9... | collective-permute-start | bytes 104 | tf_op jit(solution)/shard_map/ppermute | solution.py:15
  30.1 1.9 %collective-permute-start.7 = (s32[3,1,4]{2,1,0:T(1,128)S(1)}, s32[3,1,4]{2,1,0:T(1,128)S(1)}, u32[]{:S(2)}, u32[]{:S(2)}) collective-permute-start(s32[3,1,4]{2,1,0:T(1,128)S(1)} %get-tuple-element.90), channel_id=1, source_target_pairs={{1,0},{2,1},{3,2},{0,3},{5,4},{6,5},{7,6},{4,7},{9,8},{10,9},{11,1... | collective-permute-start | bytes 152 | tf_op jit(solution)/shard_map/ppermute | solution.py:15
  44.8 1.7 collective-permute-start.10
  48.7 16.2 %collective-permute-done.11 = f32[3,1,4,128,128]{4,3,2,1,0:T(8,128)S(1)} collective-permute-done((f32[3,1,4,128,128]{4,3,2,1,0:T(8,128)S(1)}, f32[3,1,4,128,128]{4,3,2,1,0:T(8,128)S(1)}, u32[]{:S(2)}, u32[]{:S(2)}) %collective-permute-start.11) | collective-permute-done | bytes 786464 | tf_op jit(solution)/shard_map/ppermute | solution.py:15
  65.2 1.4 gather_fusion.2
  66.6 1.4 gather_fusion.4
  68.0 1.4 gather_fusion.6
  69.4 1.4 gather_fusion.8
  70.7 1.4 gather_fusion.10
  72.1 1.4 gather_fusion.12
  73.5 1.4 gather_fusion.14
  74.9 1.4 gather_fusion.16
  76.3 2.2 %fusion.39 = f32[2,4,128,128]{3,2,1,0:T(8,128)S(1)} fusion(f32[2,4,128,128]{3,2,1,0:T(8,128)} %gather_fusion.2, pred[2]{0:T(512)(128)(4,1)S(1)} %get-tuple-element.132, f32[2,4,128,128]{3,2,1,0:T(8,128)} %bitcast.245), kind=kOutput, calls=%fused_computation.78 | convolution fusion | flops 201457664 | bytes 1179650 | tf_op jit(solution)/shard_map/xij,xtjk->xtik/dot_general | solution.py:46
  78.8 2.1 %fusion.37 = f32[2,4,128,128]{3,2,1,0:T(8,128)S(1)} fusion(f32[2,4,128,128]{3,2,1,0:T(8,128)} %gather_fusion.4, pred[2]{0:T(512)(128)(4,1)S(1)} %get-tuple-element.63, f32[2,4,128,128]{3,2,1,0:T(8,128)} %bitcast.246), kind=kOutput, calls=%fused_computation.76 | convolution fusion | flops 201457664 | bytes 1179650 | tf_op jit(solution)/shard_map/xij,xtjk->xtik/dot_general | solution.py:46
  86.8 1.9 %fusion.31 = f32[2,4,128,128]{3,2,1,0:T(8,128)} fusion(f32[2,128,128,1]{2,1,3,0:T(8,128)S(1)} %bitcast.259, f32[2,4,128,128]{3,2,1,0:T(8,128)S(1)} %copy-done.4, pred[2]{0:T(512)(128)(4,1)S(1)} %copy-done.23), kind=kOutput, calls=%fused_computation.70 | convolution fusion | flops 201457664 | bytes 1179650 | tf_op jit(solution)/shard_map/xij,xtjk->xtik/dot_general | solution.py:46
  91.4 2.5 %fusion.27 = f32[2,4,128,128]{3,2,1,0:T(8,128)} fusion(f32[2,128,128,1]{2,1,3,0:T(8,128)S(1)} %bitcast.256, f32[2,4,128,128]{3,2,1,0:T(8,128)S(1)} %copy-done.2, pred[2]{0:T(512)(128)(4,1)} %copy-done.25), kind=kOutput, calls=%fused_computation.66 | convolution fusion | flops 201457664 | bytes 1179650 | tf_op jit(solution)/shard_map/xij,xtjk->xtik/dot_general | solution.py:46
  95.2 1.9 %fusion.25 = f32[2,4,128,128]{3,2,1,0:T(8,128)S(1)} fusion(f32[2,128,128,1]{2,1,3,0:T(8,128)S(1)} %bitcast.254, f32[2,4,128,128]{3,2,1,0:T(8,128)S(1)} %copy-done.1, pred[2]{0:T(512)(128)(4,1)} %copy-done.20), kind=kOutput, calls=%fused_computation.64 | convolution fusion | flops 201457664 | bytes 1179650 | tf_op jit(solution)/shard_map/xij,xtjk->xtik/dot_general | solution.py:46
  100.2 3.1 %collective-permute-start.13 = (f32[1,2,4,128,128]{4,2,3,1,0:T(4,128)S(1)}, f32[1,2,4,128,128]{4,2,3,1,0:T(4,128)S(1)}, u32[]{:S(2)}, u32[]{:S(2)}) collective-permute-start(f32[1,2,4,128,128]{4,2,3,1,0:T(4,128)S(1)} %bitcast.241), channel_id=1, source_target_pairs={{4,0},{8,4},{12,8},{16,12},{20,16},{24,20},{28,24},{0,28},{5,1},{9... | collective-permute-start | bytes 1572872 | tf_op jit(solution)/shard_map/ppermute | solution.py:15
  103.3 21.3 %collective-permute-done.13 = f32[1,2,4,128,128]{4,2,3,1,0:T(4,128)S(1)} collective-permute-done((f32[1,2,4,128,128]{4,2,3,1,0:T(4,128)S(1)}, f32[1,2,4,128,128]{4,2,3,1,0:T(4,128)S(1)}, u32[]{:S(2)}, u32[]{:S(2)}) %collective-permute-start.13) | collective-permute-done | bytes 524320 | tf_op jit(solution)/shard_map/ppermute | solution.py:15
  128.5 16.2 %collective-permute-done.15 = f32[3,1,4,128,128]{4,2,3,1,0:T(4,128)S(1)} collective-permute-done((f32[3,1,4,128,128]{4,2,3,1,0:T(4,128)S(1)}, f32[3,1,4,128,128]{4,2,3,1,0:T(4,128)S(1)}, u32[]{:S(2)}, u32[]{:S(2)}) %collective-permute-start.15) | collective-permute-done | bytes 786464 | tf_op jit(solution)/shard_map/ppermute | solution.py:15
  145.5 1.7 gather_fusion.17
  147.3 1.6 gather_fusion.19
  148.9 1.9 %gather_fusion.21 = f32[2,4,128,128]{3,1,2,0:T(4,128)} fusion(f32[12,4,128,128]{3,1,2,0:T(4,128)S(1)} %bitcast.239, s32[1024]{0:T(1024)} %copy-done.13), kind=kCustom, calls=%fused_computation.22.clone | custom fusion | bytes 1048584 | tf_op jit(solution)/shard_map/jit(_take)/gather | solution.py:39
  150.8 1.8 gather_fusion.23
  154.0 1.6 fusion.187
  163.5 1.6 convolution_add_fusion.5
  165.2 1.6 convolution_add_fusion.4
  167.9 1.4 fusion.191
  (224 shorter events, 56.7 us)
Async XLA Ops:
  0.0 43.4 %collective-permute-start.8 = (f32[1,2,4,128,128]{4,3,2,1,0:T(8,128)}, f32[1,2,4,128,128]{4,3,2,1,0:T(8,128)S(1)}, u32[]{:S(2)}, u32[]{:S(2)}) collective-permute-start(f32[1,2,4,128,128]{4,3,2,1,0:T(8,128)} %param.7), channel_id=1, source_target_pairs={{0,4},{4,8},{8,12},{12,16},{16,20},{20,24},{24,28},{28,0},{1,5},{5... | collective-permute-start | bytes 1572872 | tf_op jit(solution)/shard_map/ppermute | solution.py:14
  2.1 42.5 %collective-permute-start.9 = (f32[1,2,4,128,128]{4,3,2,1,0:T(8,128)}, f32[1,2,4,128,128]{4,3,2,1,0:T(8,128)S(1)}, u32[]{:S(2)}, u32[]{:S(2)}) collective-permute-start(f32[1,2,4,128,128]{4,3,2,1,0:T(8,128)} %param.7), channel_id=1, source_target_pairs={{4,0},{8,4},{12,8},{16,12},{20,16},{24,20},{28,24},{0,28},{5,1},{9... | collective-permute-start | bytes 1572872 | tf_op jit(solution)/shard_map/ppermute | solution.py:15
  5.1 19.1 %collective-permute-start.4 = (s32[1,2,4]{2,1,0:T(2,128)}, s32[1,2,4]{2,1,0:T(2,128)S(1)}, u32[]{:S(2)}, u32[]{:S(2)}) collective-permute-start(s32[1,2,4]{2,1,0:T(2,128)} %param.8), channel_id=1, source_target_pairs={{0,4},{4,8},{8,12},{12,16},{16,20},{20,24},{24,28},{28,0},{1,5},{5... | collective-permute-start | bytes 104 | tf_op jit(solution)/shard_map/ppermute | solution.py:14
  5.1 25.0 %collective-permute-start.5 = (s32[1,2,4]{2,1,0:T(2,128)}, s32[1,2,4]{2,1,0:T(2,128)S(1)}, u32[]{:S(2)}, u32[]{:S(2)}) collective-permute-start(s32[1,2,4]{2,1,0:T(2,128)} %param.8), channel_id=1, source_target_pairs={{4,0},{8,4},{12,8},{16,12},{20,16},{24,20},{28,24},{0,28},{5,1},{9... | collective-permute-start | bytes 104 | tf_op jit(solution)/shard_map/ppermute | solution.py:15
  9.3 22.7 %collective-permute-start = (s32[1,2,4]{2,1,0:T(2,128)}, s32[1,2,4]{2,1,0:T(2,128)S(1)}, u32[]{:S(2)}, u32[]{:S(2)}) collective-permute-start(s32[1,2,4]{2,1,0:T(2,128)} %param.9), channel_id=1, source_target_pairs={{0,4},{4,8},{8,12},{12,16},{16,20},{20,24},{24,28},{28,0},{1,5},{5... | collective-permute-start | bytes 104 | tf_op jit(solution)/shard_map/ppermute | solution.py:14
  14.5 32.1 %copy-start.17 = (pred[2]{0:T(512)(128)(4,1)}, pred[2]{0:T(512)(128)(4,1)S(1)}, u32[]{:S(2)}) copy-start(pred[2]{0:T(512)(128)(4,1)S(1)} %get-tuple-element.43) | copy-start | bytes 10
  14.6 30.2 %copy-start.22 = (pred[2]{0:T(512)(128)(4,1)}, pred[2]{0:T(512)(128)(4,1)S(1)}, u32[]{:S(2)}) copy-start(pred[2]{0:T(512)(128)(4,1)S(1)} %get-tuple-element.48) | copy-start | bytes 10
  14.6 33.4 %copy-start.20 = (pred[2]{0:T(512)(128)(4,1)}, pred[2]{0:T(512)(128)(4,1)S(1)}, u32[]{:S(2)}) copy-start(pred[2]{0:T(512)(128)(4,1)S(1)} %get-tuple-element.33) | copy-start | bytes 10
  14.7 32.7 %copy-start.25 = (pred[2]{0:T(512)(128)(4,1)}, pred[2]{0:T(512)(128)(4,1)S(1)}, u32[]{:S(2)}) copy-start(pred[2]{0:T(512)(128)(4,1)S(1)} %get-tuple-element.38) | copy-start | bytes 10
  14.7 56.1 %copy-start.11 = (s32[1024]{0:T(1024)}, s32[1024]{0:T(1024)S(1)}, u32[]{:S(2)}) copy-start(s32[1024]{0:T(1024)S(1)} %get-tuple-element.138) | copy-start | bytes 12292
  14.7 58.8 %copy-start.13 = (s32[1024]{0:T(1024)}, s32[1024]{0:T(1024)S(1)}, u32[]{:S(2)}) copy-start(s32[1024]{0:T(1024)S(1)} %get-tuple-element.136) | copy-start | bytes 12292
  14.7 60.2 %copy-start.12 = (s32[1024]{0:T(1024)}, s32[1024]{0:T(1024)S(1)}, u32[]{:S(2)}) copy-start(s32[1024]{0:T(1024)S(1)} %get-tuple-element.135) | copy-start | bytes 12292
  24.2 9.6 %collective-permute-start.1 = (s32[1,2,4]{2,1,0:T(2,128)}, s32[1,2,4]{2,1,0:T(2,128)S(1)}, u32[]{:S(2)}, u32[]{:S(2)}) collective-permute-start(s32[1,2,4]{2,1,0:T(2,128)} %param.9), channel_id=1, source_target_pairs={{4,0},{8,4},{12,8},{16,12},{20,16},{24,20},{28,24},{0,28},{5,1},{9... | collective-permute-start | bytes 104 | tf_op jit(solution)/shard_map/ppermute | solution.py:15
  30.1 4.3 %collective-permute-start.7 = (s32[3,1,4]{2,1,0:T(1,128)S(1)}, s32[3,1,4]{2,1,0:T(1,128)S(1)}, u32[]{:S(2)}, u32[]{:S(2)}) collective-permute-start(s32[3,1,4]{2,1,0:T(1,128)S(1)} %get-tuple-element.90), channel_id=1, source_target_pairs={{1,0},{2,1},{3,2},{0,3},{5,4},{6,5},{7,6},{4,7},{9,8},{10,9},{11,1... | collective-permute-start | bytes 152 | tf_op jit(solution)/shard_map/ppermute | solution.py:15
  32.0 3.7 %collective-permute-start.6 = (s32[3,1,4]{2,1,0:T(1,128)S(1)}, s32[3,1,4]{2,1,0:T(1,128)S(1)}, u32[]{:S(2)}, u32[]{:S(2)}) collective-permute-start(s32[3,1,4]{2,1,0:T(1,128)S(1)} %get-tuple-element.89), channel_id=1, source_target_pairs={{0,1},{1,2},{2,3},{3,0},{4,5},{5,6},{6,7},{7,4},{8,9},{9,10},{10,1... | collective-permute-start | bytes 152 | tf_op jit(solution)/shard_map/ppermute | solution.py:14
  33.9 3.8 %collective-permute-start.3 = (s32[3,1,4]{2,1,0:T(1,128)S(1)}, s32[3,1,4]{2,1,0:T(1,128)S(1)}, u32[]{:S(2)}, u32[]{:S(2)}) collective-permute-start(s32[3,1,4]{2,1,0:T(1,128)S(1)} %get-tuple-element.88), channel_id=1, source_target_pairs={{1,0},{2,1},{3,2},{0,3},{5,4},{6,5},{7,6},{4,7},{9,8},{10,9},{11,1... | collective-permute-start | bytes 152 | tf_op jit(solution)/shard_map/ppermute | solution.py:15
  34.4 3.3 %collective-permute-start.2 = (s32[3,1,4]{2,1,0:T(1,128)S(1)}, s32[3,1,4]{2,1,0:T(1,128)S(1)}, u32[]{:S(2)}, u32[]{:S(2)}) collective-permute-start(s32[3,1,4]{2,1,0:T(1,128)S(1)} %get-tuple-element.87), channel_id=1, source_target_pairs={{0,1},{1,2},{2,3},{3,0},{4,5},{5,6},{6,7},{7,4},{8,9},{9,10},{10,1... | collective-permute-start | bytes 152 | tf_op jit(solution)/shard_map/ppermute | solution.py:14
  44.8 20.1 %collective-permute-start.11 = (f32[3,1,4,128,128]{4,3,2,1,0:T(8,128)S(1)}, f32[3,1,4,128,128]{4,3,2,1,0:T(8,128)S(1)}, u32[]{:S(2)}, u32[]{:S(2)}) collective-permute-start(f32[3,1,4,128,128]{4,3,2,1,0:T(8,128)S(1)} %get-tuple-element.74), channel_id=1, source_target_pairs={{1,0},{2,1},{3,2},{0,3},{5,4},{6,5},{7,6},{4,7},{9,8},{10,9},{11,1... | collective-permute-start | bytes 2359304 | tf_op jit(solution)/shard_map/ppermute | solution.py:15
  44.8 20.0 %collective-permute-start.10 = (f32[3,1,4,128,128]{4,3,2,1,0:T(8,128)S(1)}, f32[3,1,4,128,128]{4,3,2,1,0:T(8,128)S(1)}, u32[]{:S(2)}, u32[]{:S(2)}) collective-permute-start(f32[3,1,4,128,128]{4,3,2,1,0:T(8,128)S(1)} %get-tuple-element.73), channel_id=1, source_target_pairs={{0,1},{1,2},{2,3},{3,0},{4,5},{5,6},{6,7},{7,4},{8,9},{9,10},{10,1... | collective-permute-start | bytes 2359304 | tf_op jit(solution)/shard_map/ppermute | solution.py:14
  86.8 8.3 %copy-start.1 = (f32[2,4,128,128]{3,2,1,0:T(8,128)S(1)}, f32[2,4,128,128]{3,2,1,0:T(8,128)}, u32[]{:S(2)}) copy-start(f32[2,4,128,128]{3,2,1,0:T(8,128)} %gather_fusion.16) | copy-start | bytes 1572868
  100.1 26.8 %copy-start.33 = (s32[2,4]{1,0:T(2,128)S(1)}, s32[2,4]{1,0:T(2,128)}, u32[]{:S(2)}) copy-start(s32[2,4]{1,0:T(2,128)} %get-tuple-element.117) | copy-start | bytes 100
  100.1 26.8 %copy-start.34 = (s32[2,4]{1,0:T(2,128)S(1)}, s32[2,4]{1,0:T(2,128)}, u32[]{:S(2)}) copy-start(s32[2,4]{1,0:T(2,128)} %get-tuple-element.118) | copy-start | bytes 100
  100.1 26.8 %copy-start.35 = (s32[2,4]{1,0:T(2,128)S(1)}, s32[2,4]{1,0:T(2,128)}, u32[]{:S(2)}) copy-start(s32[2,4]{1,0:T(2,128)} %get-tuple-element.113) | copy-start | bytes 100
  100.1 26.8 %copy-start.36 = (s32[2,4]{1,0:T(2,128)S(1)}, s32[2,4]{1,0:T(2,128)}, u32[]{:S(2)}) copy-start(s32[2,4]{1,0:T(2,128)} %get-tuple-element.114) | copy-start | bytes 100
  100.2 26.7 %copy-start.37 = (s32[2,4]{1,0:T(2,128)S(1)}, s32[2,4]{1,0:T(2,128)}, u32[]{:S(2)}) copy-start(s32[2,4]{1,0:T(2,128)} %get-tuple-element.109) | copy-start | bytes 100
  100.2 26.7 %copy-start.38 = (s32[2,4]{1,0:T(2,128)S(1)}, s32[2,4]{1,0:T(2,128)}, u32[]{:S(2)}) copy-start(s32[2,4]{1,0:T(2,128)} %get-tuple-element.110) | copy-start | bytes 100
  100.2 26.7 %copy-start.39 = (s32[2,4]{1,0:T(2,128)S(1)}, s32[2,4]{1,0:T(2,128)}, u32[]{:S(2)}) copy-start(s32[2,4]{1,0:T(2,128)} %get-tuple-element.105) | copy-start | bytes 100
  100.2 26.7 %copy-start.40 = (s32[2,4]{1,0:T(2,128)S(1)}, s32[2,4]{1,0:T(2,128)}, u32[]{:S(2)}) copy-start(s32[2,4]{1,0:T(2,128)} %get-tuple-element.106) | copy-start | bytes 100
  100.2 24.4 %collective-permute-start.13 = (f32[1,2,4,128,128]{4,2,3,1,0:T(4,128)S(1)}, f32[1,2,4,128,128]{4,2,3,1,0:T(4,128)S(1)}, u32[]{:S(2)}, u32[]{:S(2)}) collective-permute-start(f32[1,2,4,128,128]{4,2,3,1,0:T(4,128)S(1)} %bitcast.241), channel_id=1, source_target_pairs={{4,0},{8,4},{12,8},{16,12},{20,16},{24,20},{28,24},{0,28},{5,1},{9... | collective-permute-start | bytes 1572872 | tf_op jit(solution)/shard_map/ppermute | solution.py:15
  103.2 21.4 %collective-permute-start.12 = (f32[1,2,4,128,128]{4,2,3,1,0:T(4,128)S(1)}, f32[1,2,4,128,128]{4,2,3,1,0:T(4,128)S(1)}, u32[]{:S(2)}, u32[]{:S(2)}) collective-permute-start(f32[1,2,4,128,128]{4,2,3,1,0:T(4,128)S(1)} %bitcast.242), channel_id=1, source_target_pairs={{0,4},{4,8},{8,12},{12,16},{16,20},{20,24},{24,28},{28,0},{1,5},{5... | collective-permute-start | bytes 1572872 | tf_op jit(solution)/shard_map/ppermute | solution.py:14
  125.1 19.6 %collective-permute-start.15 = (f32[3,1,4,128,128]{4,2,3,1,0:T(4,128)S(1)}, f32[3,1,4,128,128]{4,2,3,1,0:T(4,128)S(1)}, u32[]{:S(2)}, u32[]{:S(2)}) collective-permute-start(f32[3,1,4,128,128]{4,2,3,1,0:T(4,128)S(1)} %get-tuple-element.72), channel_id=1, source_target_pairs={{1,0},{2,1},{3,2},{0,3},{5,4},{6,5},{7,6},{4,7},{9,8},{10,9},{11,1... | collective-permute-start | bytes 2359304 | tf_op jit(solution)/shard_map/ppermute | solution.py:15
  126.4 18.4 %collective-permute-start.14 = (f32[3,1,4,128,128]{4,2,3,1,0:T(4,128)S(1)}, f32[3,1,4,128,128]{4,2,3,1,0:T(4,128)S(1)}, u32[]{:S(2)}, u32[]{:S(2)}) collective-permute-start(f32[3,1,4,128,128]{4,2,3,1,0:T(4,128)S(1)} %get-tuple-element.71), channel_id=1, source_target_pairs={{0,1},{1,2},{2,3},{3,0},{4,5},{5,6},{6,7},{7,4},{8,9},{9,10},{10,1... | collective-permute-start | bytes 2359304 | tf_op jit(solution)/shard_map/ppermute | solution.py:14
  (27 other events, 128.2 us)
where the time goes:
time: 179 us; the launch traced here: 177 us
  waiting for transfers between devices  63.7 us (36%)
  local copies, waits for them, and re-layouts  40.9 us (23%)
  matrix products  32.6 us (18%)
  starting transfers between devices  25.5 us (14%)
  other arithmetic  13.3 us (7%)
    ppermute x8, waiting for transfers between devices, extended(): after = lax.ppermute(initial, axis, down)  54.2 us
    dot_general x16, matrix products, local_product(): jnp.einsum('xij,xtjk->xtik', flat_left[:, slot_idx], near_blocks, precisi...  20.3 us
    ppermute x8, starting transfers between devices, extended(): after = lax.ppermute(initial, axis, down)  18.7 us
    gather x12, local copies, waits for them, and re-layouts, local_product(): near_blocks = jnp.take(flat_right, target, axis=0)  18 us
    dot_general x16, matrix products, local_product(): jnp.einsum('xtu,xtik->xuik', matches, products, precision=lax.Precision.H...  12.3 us
    dot_general x16, local copies, waits for them, and re-layouts, local_product(): jnp.einsum('xij,xtjk->xtik', flat_left[:, slot_idx], near_blocks, precisi...  9.91 us
    ppermute x8, waiting for transfers between devices, extended(): before = lax.ppermute(last, axis, up)  9.53 us
    ppermute x8, starting transfers between devices, extended(): before = lax.ppermute(last, axis, up)  6.81 us
  transfers between devices with their start and end apart: 16, of which 5 were waited for; matrix products, arithmetic and copies ran while one was open for 11% of the time, Pallas kernels for 0%

commit v1 on v0

v1 whole, which is shorter than its diff:
```python
import jax
import jax.numpy as jnp
from jax import lax
from jax.experimental import pallas as pl
from jax.experimental.pallas import tpu as pltpu
from jax.sharding import PartitionSpec as P

SLOTS = 4
SITES = 2
WIDE = SITES + 2
CHUNKS = 2
ZERO_BLOCK = 3 * WIDE * SLOTS
MESH = pl.DeviceIdType.MESH


def split(x):
    high = x.astype(jnp.bfloat16)
    low = (x - high.astype(jnp.float32)).astype(jnp.bfloat16)
    return high, low


def kernel(
    rows, cols, codes_ref, density_ref, out_ref,
    near0, near1, codes, scalars, table, right_high, right_low,
    send_sem, recv_sem, code_send, code_recv, local_sem,
):
    block = out_ref.shape[-1]
    row, col = lax.axis_index("row"), lax.axis_index("col")
    odd = lax.rem(row, 2)
    pair = row + 1 - 2 * odd
    onward = lax.rem(row + 2 - 4 * odd + rows, rows)
    backward = lax.rem(row - 2 + 4 * odd + rows, rows)
    left, right = lax.rem(col + cols - 1, cols), lax.rem(col + 1, cols)
    paired, handed = 2 - 2 * odd, 2 * odd
    own = WIDE + 1

    load = pltpu.make_async_copy(
        density_ref, near0.at[pl.ds(own * SLOTS, SITES * SLOTS)], local_sem
    )
    load.start()
    for j in range(SITES):
        codes[own + j] = codes_ref[j]
    near0[ZERO_BLOCK] = jnp.zeros((block, block), jnp.float32)
    near1[ZERO_BLOCK] = jnp.zeros((block, block), jnp.float32)

    barrier = pltpu.get_barrier_semaphore()
    others = [(pair, col), (onward, col), (backward, col), (row, left), (row, right)]
    for other in others:
        pl.semaphore_signal(barrier, inc=1, device_id=other, device_id_type=MESH)
    pl.semaphore_wait(barrier, len(others))

    def send(ref, source, target, size, sems, index, device):
        return pltpu.make_async_remote_copy(
            src_ref=ref.at[pl.ds(source, size)],
            dst_ref=ref.at[pl.ds(target, size)],
            send_sem=sems[0].at[index],
            recv_sem=sems[1].at[index],
            device_id=device,
            device_id_type=MESH,
        )

    def code_copy(index, source, target, size, device):
        return send(codes, source, target, size, (code_send, code_recv), index, device)

    part = SLOTS // CHUNKS

    def block_copy(step, kind, chunk, source, target, device):
        near = (near0, near1)[step]
        index = (step * 10 + kind) * CHUNKS + chunk
        return send(
            near, source * SLOTS + chunk * part, target * SLOTS + chunk * part, part,
            (send_sem, recv_sem), index, device,
        )

    def to_pair(step, j, chunk):
        return block_copy(step, j, chunk, own + j, handed * WIDE + 1 + j, (pair, col))

    def hand_on(step, j, chunk):
        return block_copy(
            step, 2 + j, chunk, paired * WIDE + 1 + j, handed * WIDE + 1 + j, (onward, col)
        )

    def sideways(step, place, j, chunk):
        window_row = (1, paired, handed)[place]
        device = (row, (left, right)[j])
        return block_copy(
            step, 4 + 2 * place + j, chunk,
            window_row * WIDE + 1 + j, window_row * WIDE + (WIDE - 1, 0)[j], device,
        )

    def begin(step, j):
        for chunk in range(CHUNKS):
            to_pair(step, j, chunk).start()
            sideways(step, 0, j, chunk).start()

    def relay(step):
        for j in range(SITES):
            for chunk in range(CHUNKS):
                to_pair(step, j, chunk).wait_recv()
                hand_on(step, j, chunk).start()
                sideways(step, 1, j, chunk).start()
        for j in range(SITES):
            for chunk in range(CHUNKS):
                hand_on(step, j, chunk).wait_recv()
                sideways(step, 2, j, chunk).start()

    def finish(step):
        for j in range(SITES):
            for chunk in range(CHUNKS):
                for place in range(3):
                    sideways(step, place, j, chunk).wait_recv()
        for j in range(SITES):
            for chunk in range(CHUNKS):
                to_pair(step, j, chunk).wait_send()
                hand_on(step, j, chunk).wait_send()
                for place in range(3):
                    sideways(step, place, j, chunk).wait_send()

    codes_pair = code_copy(0, own, handed * WIDE + 1, SITES, (pair, col))
    codes_on = code_copy(1, paired * WIDE + 1, handed * WIDE + 1, SITES, (onward, col))
    codes_side = [
        [
            code_copy(
                2 + 2 * place + j, window_row * WIDE + 1 + j,
                window_row * WIDE + (WIDE - 1, 0)[j], 1, (row, (left, right)[j]),
            )
            for j in range(SITES)
        ]
        for place, window_row in enumerate((1, paired, handed))
    ]
    codes_pair.start()
    for copy in codes_side[0]:
        copy.start()
    load.wait()
    for j in range(SITES):
        begin(0, j)
    codes_pair.wait_recv()
    codes_on.start()
    for copy in codes_side[1]:
        copy.start()
    codes_on.wait_recv()
    for copy in codes_side[2]:
        copy.start()
    relay(0)
    for place in range(3):
        for copy in codes_side[place]:
            copy.wait()
    codes_pair.wait_send()
    codes_on.wait_send()
    to_scalars = pltpu.make_async_copy(codes, scalars, local_sem)
    to_scalars.start()
    to_scalars.wait()

    def fill(number, left_base, right_base):
        for j in range(SITES):
            for s in range(SLOTS):
                first = scalars[own + j, 0, left_base + s]
                site = own + j + scalars[own + j, 0, 8 + left_base + s]
                second = [scalars[site, 0, right_base + t] for t in range(SLOTS)]
                for u in range(SLOTS):
                    rest = scalars[own + j, 0, 4 + u] - first
                    found = jnp.int32(ZERO_BLOCK)
                    for t in range(SLOTS):
                        found = jnp.where(second[t] == rest, site * SLOTS + t, found)
                    table[((number * SITES + j) * SLOTS + s) * SLOTS + u] = found

    fill(0, 0, 0)
    fill(1, 4, 0)
    fill(2, 4, 4)
    finish(0)

    def gather(near, number, j):
        for s in range(SLOTS):
            for u in range(SLOTS):
                found = table[((number * SITES + j) * SLOTS + s) * SLOTS + u]
                high, low = split(near[found])
                place = (pl.ds(s * block, block), pl.ds(u * block, block))
                right_high[place] = high
                right_low[place] = low

    def product(left_blocks):
        high, low = split(left_blocks)
        dot = lambda a, b: jnp.dot(a, b, preferred_element_type=jnp.float32)
        return (
            dot(high, right_low[...]) + dot(low, right_high[...]) + dot(high, right_high[...])
        )

    def purify(near, numbers, j):
        gather(near, numbers[0], j)
        mine = jnp.concatenate(
            [near[(own + j) * SLOTS + s] for s in range(SLOTS)], axis=1
        )
        square = product(mine)
        if numbers[1] != numbers[0]:
            gather(near, numbers[1], j)
        return 3.0 * square - 2.0 * product(square)

    for j in range(SITES):
        result = purify(near0, (0, 1), j)
        for u in range(SLOTS):
            near1[(own + j) * SLOTS + u] = result[:, u * block:(u + 1) * block]
        begin(1, j)
    relay(1)
    finish(1)
    for j in range(SITES):
        result = purify(near1, (2, 2), j)
        for u in range(SLOTS):
            out_ref[j * SLOTS + u] = result[:, u * block:(u + 1) * block]


def on_device(rows, cols, density, pattern, retained):
    block = density.shape[-1]
    both = jnp.concatenate([pattern, retained], axis=-1).reshape(SITES, 2 * SLOTS)
    step_a, step_b = both // 3 - 1, both % 3 - 1
    lanes = jnp.concatenate([5 * step_a + step_b, WIDE * step_a + step_b], axis=-1)
    codes = jnp.zeros((SITES, 8, 128), jnp.int32).at[:, 0, :4 * SLOTS].set(lanes)
    window = (ZERO_BLOCK + 1, block, block)
    out = pl.pallas_call(
        lambda *refs: kernel(rows, cols, *refs),
        out_shape=jax.ShapeDtypeStruct((SITES * SLOTS, block, block), jnp.float32),
        in_specs=[
            pl.BlockSpec(memory_space=pltpu.VMEM),
            pl.BlockSpec(memory_space=pl.ANY),
        ],
        out_specs=pl.BlockSpec(memory_space=pltpu.VMEM),
        scratch_shapes=[
            pltpu.VMEM(window, jnp.float32),
            pltpu.VMEM(window, jnp.float32),
            pltpu.VMEM((3 * WIDE, 8, 128), jnp.int32),
            pltpu.SMEM((3 * WIDE, 8, 128), jnp.int32),
            pltpu.SMEM((3 * SITES * SLOTS * SLOTS,), jnp.int32),
            pltpu.VMEM((SLOTS * block, SLOTS * block), jnp.bfloat16),
            pltpu.VMEM((SLOTS * block, SLOTS * block), jnp.bfloat16),
            pltpu.SemaphoreType.DMA((20 * CHUNKS,)),
            pltpu.SemaphoreType.DMA((20 * CHUNKS,)),
            pltpu.SemaphoreType.DMA((8,)),
            pltpu.SemaphoreType.DMA((8,)),
            pltpu.SemaphoreType.DMA,
        ],
        compiler_params=pltpu.CompilerParams(
            collective_id=0, has_side_effects=True, vmem_limit_bytes=32 * 1024 * 1024
        ),
    )(codes, density.reshape((SITES * SLOTS, block, block)))
    return out.reshape(density.shape)


def solution(mesh):
    rows, cols = mesh.shape["row"], mesh.shape["col"]
    return jax.shard_map(
        lambda *args: on_device(rows, cols, *args),
        mesh=mesh,
        in_specs=(P("row", "col", None, None, None), P("row", "col", None), P("row", "col", None)),
        out_specs=P("row", "col", None, None, None),
        check_vma=False,
    )
```

time: 179 us -> 54.4 us (0.30)
  the two profiles are of different devices: /device:TPU:1 before, /device:TPU:0 now
where the time goes in v1:
time: 54.4 us; the launch traced here: 54.2 us
  Pallas kernels  50.9 us (94%)
  local copies, waits for them, and re-layouts  2.52 us (5%)
  other arithmetic  0.85 us (2%)
    pallas_call x1, Pallas kernels, on_device(): pl.pallas_call(lambda *refs: kernel(rows, cols, *refs), out_shape=jax.Sha...  50.9 us
    unnamed x5, local copies, waits for them, and re-layouts  2.52 us

profile of v1, /device:TPU:0, one launch (start us, length us, event | category | flops | bytes accessed | tf_op | source)
XLA Modules:
  0.0 54.2 jit_solution(1476284867342686292)
XLA Ops:
  0.0 0.0 copy-start.1
  0.0 0.7 %copy-done.1 = s32[1,2,4]{2,1,0:T(2,128)S(1)} copy-done((s32[1,2,4]{2,1,0:T(2,128)S(1)}, s32[1,2,4]{2,1,0:T(2,128)}, u32[]{:S(2)}) %copy-start.1) | copy-done | bytes 56
  0.7 0.8 %multiply_add_fusion.1 = (s32[2,8]{1,0:T(2,128)S(1)}, s32[2,8]{1,0:T(2,128)S(1)}, s32[2,8]{1,0:T(2,128)S(1)}) fusion(s32[1,2,4]{2,1,0:T(2,128)S(1)} %copy-done.1, s32[1,2,4]{2,1,0:T(2,128)} %param.6), kind=kLoop, calls=%fused_computation.9 | loop fusion | flops 272 | bytes 256 | tf_op jit(solution)/shard_map/add | solution.py:215
  1.5 0.1 pad_add_fusion.1
  1.5 0.0 copy-start
  1.5 1.0 %copy-done = f32[1,2,4,128,128]{4,3,2,1,0:T(8,128)S(1)} copy-done((f32[1,2,4,128,128]{4,3,2,1,0:T(8,128)S(1)}, f32[1,2,4,128,128]{4,3,2,1,0:T(8,128)}, u32[]{:S(2)}) %copy-start) | copy-done | bytes 524312
  2.6 50.9 %shard_map.37 = f32[8,128,128]{2,1,0:T(8,128)S(1)} custom-call(s32[2,8,128]{2,1,0:T(8,128)S(1)} %scatter.4.refs_0_, f32[8,128,128]{2,1,0:T(8,128)S(1)} %bitcast.25), custom_call_target="tpu_custom_call" | custom-call | tf_op jit(solution)/shard_map/pallas_call | solution.py:218
  53.5 0.8 %copy.6 = f32[1,2,4,128,128]{4,3,2,1,0:T(8,128)} copy(f32[1,2,4,128,128]{4,3,2,1,0:T(8,128)S(1)} %bitcast.24) | data formatting | bytes 1048576
  (2 shorter events, 0.0 us)
Async XLA Ops:
  0.0 0.7 %copy-start.1 = (s32[1,2,4]{2,1,0:T(2,128)S(1)}, s32[1,2,4]{2,1,0:T(2,128)}, u32[]{:S(2)}) copy-start(s32[1,2,4]{2,1,0:T(2,128)} %param.7) | copy-start | bytes 100
  1.5 1.0 %copy-start = (f32[1,2,4,128,128]{4,3,2,1,0:T(8,128)S(1)}, f32[1,2,4,128,128]{4,3,2,1,0:T(8,128)}, u32[]{:S(2)}) copy-start(f32[1,2,4,128,128]{4,3,2,1,0:T(8,128)} %param.5) | copy-start | bytes 1572868

commit v2 on v1

v2 whole, which is shorter than its diff:
```python
import jax
import jax.numpy as jnp
from jax import lax
from jax.experimental import pallas as pl
from jax.experimental.pallas import tpu as pltpu
from jax.sharding import PartitionSpec as P

SLOTS = 4
SITES = 2
WIDE = SITES + 2
CHUNKS = 2
ZERO_BLOCK = 3 * WIDE * SLOTS
FLIPPED = ZERO_BLOCK + 1
MESH = pl.DeviceIdType.MESH


def split(x):
    high = x.astype(jnp.bfloat16)
    low = (x - high.astype(jnp.float32)).astype(jnp.bfloat16)
    return high, low


def kernel(
    rows, cols, pattern_ref, retained_ref, density_ref, out_ref,
    near0, near1, held, packed, codes, scalars, table, right_high, right_low,
    send_sem, recv_sem, code_send, code_recv, local_sem,
):
    block = out_ref.shape[-1]
    row, col = lax.axis_index("row"), lax.axis_index("col")
    odd, core = lax.rem(row, 2), lax.rem(col, 2)
    pair = row + 1 - 2 * odd
    onward = lax.rem(row + 2 - 4 * odd + rows, rows)
    backward = lax.rem(row - 2 + 4 * odd + rows, rows)
    beside = (lax.rem(col + cols - 1 + 2 * core, cols), lax.rem(col + cols + 1 - 2 * core, cols))
    here, there = (1 + core, 2 - core), (WIDE - 1 - 3 * core, 3 * core)
    outer_in = 3 * core
    paired, handed = 2 - 2 * odd, 2 * odd
    window_rows = (1, paired, handed)
    own = WIDE + 1

    load = pltpu.make_async_copy(
        density_ref, near0.at[pl.ds(own * SLOTS, SITES * SLOTS)], local_sem.at[0]
    )
    load.start()
    load_held = pltpu.make_async_copy(
        density_ref, held.at[pl.ds(0, SITES * SLOTS)], local_sem.at[2]
    )
    load_held.start()
    held[SITES * SLOTS] = jnp.zeros((block, block), jnp.float32)
    for j in range(SITES):
        codes[own + j] = jnp.zeros(codes.shape[1:], jnp.int32)
        for k, ref in enumerate((pattern_ref, retained_ref)):
            code = ref[j:j + 1, :]
            third = jnp.where(code >= 6, 2, jnp.where(code >= 3, 1, 0))
            codes[own + j, k:k + 1, 0:SLOTS] = code + 2 * third - 6
            codes[own + j, 2 + k:3 + k, 0:SLOTS] = code + third - 5
    own_scalars = pltpu.make_async_copy(
        codes.at[pl.ds(own, SITES)], scalars.at[pl.ds(own, SITES)], local_sem.at[1]
    )
    own_scalars.start()
    near0[ZERO_BLOCK] = jnp.zeros((block, block), jnp.float32)
    near1[ZERO_BLOCK] = jnp.zeros((block, block), jnp.float32)

    barrier = pltpu.get_barrier_semaphore()
    others = [(pair, col), (onward, col), (backward, col), (row, beside[0]), (row, beside[1])]
    for other in others:
        pl.semaphore_signal(barrier, inc=1, device_id=other, device_id_type=MESH)
    pl.semaphore_wait(barrier, len(others))

    def send(from_ref, ref, source, target, size, sems, index, device):
        return pltpu.make_async_remote_copy(
            src_ref=from_ref.at[pl.ds(source, size)],
            dst_ref=ref.at[pl.ds(target, size)],
            send_sem=sems[0].at[index],
            recv_sem=sems[1].at[index],
            device_id=device,
            device_id_type=MESH,
        )

    def code_copy(index, source, target, size, device):
        return send(codes, codes, source, target, size, (code_send, code_recv), index, device)

    def block_copy(step, kind, chunk, part, source, target, device, from_ref=None, start=None):
        near = (near0, near1)[step]
        index = (step * 11 + kind) * CHUNKS + chunk
        first = source * SLOTS + chunk * part if start is None else start
        return send(
            near if from_ref is None else from_ref, near, first, target * SLOTS + chunk * part,
            part, (send_sem, recv_sem), index, device,
        )

    parts = (2 // CHUNKS, SLOTS // CHUNKS)

    def to_pair(step, role, chunk):
        column, part = here[role], parts[step]
        target = handed * WIDE + column
        if step == 0:
            start = (column - 1) * 2 + chunk * part
            return block_copy(0, role, chunk, part, 0, target, (pair, col), packed, start)
        return block_copy(1, role, chunk, part, WIDE + column, target, (pair, col))

    def hand_on(step, role, chunk):
        column = (here + (outer_in,))[role]
        return block_copy(
            step, 2 + role, chunk, parts[step],
            paired * WIDE + column, handed * WIDE + column, (onward, col),
        )

    def sideways(step, place, role, chunk):
        part = SLOTS // CHUNKS if place == 0 else parts[step]
        base = window_rows[place] * WIDE
        return block_copy(
            step, 5 + 2 * place + role, chunk, part,
            base + here[role], base + there[role], (row, beside[role]),
        )

    def begin(step, role):
        for chunk in range(CHUNKS):
            to_pair(step, role, chunk).start()
        for chunk in range(CHUNKS):
            sideways(step, 0, role, chunk).start()

    def relay(step):
        for role in range(2):
            for chunk in range(CHUNKS):
                to_pair(step, role, chunk).wait_recv()
                hand_on(step, role, chunk).start()
                sideways(step, 1, role, chunk).start()
        hand_on(step, 0, 0).wait_recv()
        sideways(step, 2, 0, 0).start()
        sideways(step, 1, 0, 1).wait_recv()
        hand_on(step, 2, 1).start()
        hand_on(step, 0, 1).wait_recv()
        for chunk in range(CHUNKS):
            hand_on(step, 1, chunk).wait_recv()
            sideways(step, 2, 1, chunk).start()

    def finish(step):
        for chunk in range(CHUNKS):
            for role in range(2):
                sideways(step, 0, role, chunk).wait_recv()
        sideways(step, 1, 0, 0).wait_recv()
        sideways(step, 2, 0, 0).wait_recv()
        hand_on(step, 2, 1).wait_recv()
        for chunk in range(CHUNKS):
            for place in (1, 2):
                sideways(step, place, 1, chunk).wait_recv()
        for chunk in range(CHUNKS):
            for role in range(2):
                to_pair(step, role, chunk).wait_send()
                hand_on(step, role, chunk).wait_send()
                for place in range(3):
                    if (place, role, chunk) != (2, 0, 1):
                        sideways(step, place, role, chunk).wait_send()
        hand_on(step, 2, 1).wait_send()

    def flip(source, target):
        near0[target] = near0[source].T

    codes_pair = code_copy(0, own, handed * WIDE + 1, SITES, (pair, col))
    codes_on = code_copy(1, paired * WIDE + 1, handed * WIDE + 1, SITES, (onward, col))
    codes_side = [
        [
            code_copy(
                2 + 2 * place + role, window_row * WIDE + here[role],
                window_row * WIDE + there[role], 1, (row, beside[role]),
            )
            for role in range(2)
        ]
        for place, window_row in enumerate(window_rows)
    ]
    codes_pair.start()
    for copy in codes_side[0]:
        copy.start()
    own_scalars.wait()
    load_held.wait()
    for j in range(SITES):
        packed[2 * j] = held[j * SLOTS]
        found = jnp.int32(SITES * SLOTS)
        for t in range(1, SLOTS):
            found = jnp.where(scalars[own + j, 0, t] == 1, j * SLOTS + t, found)
        packed[2 * j + 1] = held[found]
    load.wait()
    for role in range(2):
        begin(0, role)
    for j in range(SITES):
        for t in range(1, SLOTS):
            flip((own + j) * SLOTS + t, FLIPPED + (1 + j) * SLOTS + t)
    codes_pair.wait_recv()
    codes_on.start()
    for copy in codes_side[1]:
        copy.start()
    codes_on.wait_recv()
    for copy in codes_side[2]:
        copy.start()
    relay(0)
    for place in range(3):
        for copy in codes_side[place]:
            copy.wait()
    codes_pair.wait_send()
    codes_on.wait_send()
    to_scalars = pltpu.make_async_copy(codes, scalars, local_sem.at[1])
    to_scalars.start()
    to_scalars.wait()

    def fill(number, left_row, right_row, symmetric):
        def one(j, s):
            first = scalars[own + j, left_row, s]
            site = own + j + scalars[own + j, 2 + left_row, s]
            second = [scalars[site, right_row, t] for t in range(SLOTS)]
            in_row = (site >= WIDE) & (site < 2 * WIDE)
            for u in range(SLOTS):
                rest = scalars[own + j, 1, u] - first
                found = jnp.int32(ZERO_BLOCK)
                for t in range(SLOTS):
                    found = jnp.where(second[t] == rest, site * SLOTS + t, found)
                if symmetric:
                    last = own + j + scalars[own + j, 3, u]
                    reverse = jnp.int32(ZERO_BLOCK)
                    for t in range(SLOTS):
                        reverse = jnp.where(
                            scalars[last, right_row, t] == -rest,
                            FLIPPED + (last - WIDE) * SLOTS + t, reverse,
                        )
                    last_in_row = (last >= WIDE) & (last < 2 * WIDE)
                    edge = FLIPPED + WIDE * SLOTS + jnp.where(last < WIDE, last, last - WIDE)
                    sent = jnp.where(
                        rest == 0, site * SLOTS,
                        jnp.where(rest == 1, site * SLOTS + 1, jnp.where(rest == -1, edge, reverse)),
                    )
                    usable = (found != ZERO_BLOCK) & (
                        last_in_row | (rest == 0) | (rest == 1) | (rest == -1)
                    )
                    sent = jnp.where(usable, sent, ZERO_BLOCK)
                    found = jnp.where(in_row, found, sent)
                table[((number * SITES + j) * SLOTS + s) * SLOTS + u] = found

        for j in range(SITES):
            for s in range(SLOTS):
                one(j, s)

    fill(0, 0, 0, True)
    fill(1, 1, 0, True)
    fill(2, 1, 1, False)
    finish(0)
    for column in (0, WIDE - 1):
        for t in range(1, SLOTS):
            flip((WIDE + column) * SLOTS + t, FLIPPED + column * SLOTS + t)
    for k in range(2):
        for column in range(WIDE - 1):
            flip((2 * k * WIDE + column) * SLOTS + 1, FLIPPED + (SLOTS + k) * WIDE + column)

    def gather(near, number, j):
        for s in range(SLOTS):
            for u in range(SLOTS):
                found = table[((number * SITES + j) * SLOTS + s) * SLOTS + u]
                high, low = split(near[found])
                place = (pl.ds(s * block, block), pl.ds(u * block, block))
                right_high[place] = high
                right_low[place] = low

    def product(left_blocks):
        high, low = split(left_blocks)
        dot = lambda a, b: jnp.dot(a, b, preferred_element_type=jnp.float32)
        return (
            dot(high, right_low[...]) + dot(low, right_high[...]) + dot(high, right_high[...])
        )

    def purify(near, numbers, j):
        gather(near, numbers[0], j)
        mine = jnp.concatenate(
            [near[(own + j) * SLOTS + s] for s in range(SLOTS)], axis=1
        )
        square = product(mine)
        if numbers[1] != numbers[0]:
            gather(near, numbers[1], j)
        return 3.0 * square - 2.0 * product(square)

    for role in range(2):
        j = here[role] - 1
        result = purify(near0, (0, 1), j)
        for u in range(SLOTS):
            near1[(own + j) * SLOTS + u] = result[:, u * block:(u + 1) * block]
        begin(1, role)
    relay(1)
    finish(1)
    for j in range(SITES):
        result = purify(near1, (2, 2), j)
        for u in range(SLOTS):
            out_ref[j * SLOTS + u] = result[:, u * block:(u + 1) * block]


def on_device(rows, cols, density, pattern, retained):
    block = density.shape[-1]
    vmem = pl.BlockSpec(memory_space=pltpu.VMEM)
    out = pl.pallas_call(
        lambda *refs: kernel(rows, cols, *refs),
        out_shape=jax.ShapeDtypeStruct((SITES * SLOTS, block, block), jnp.float32),
        in_specs=[vmem, vmem, pl.BlockSpec(memory_space=pl.ANY)],
        out_specs=vmem,
        scratch_shapes=[
            pltpu.VMEM((FLIPPED + WIDE * SLOTS + 2 * WIDE, block, block), jnp.float32),
            pltpu.VMEM((ZERO_BLOCK + 1, block, block), jnp.float32),
            pltpu.VMEM((SITES * SLOTS + 1, block, block), jnp.float32),
            pltpu.VMEM((2 * SITES, block, block), jnp.float32),
            pltpu.VMEM((3 * WIDE, 8, 128), jnp.int32),
            pltpu.SMEM((3 * WIDE, 8, 128), jnp.int32),
            pltpu.SMEM((3 * SITES * SLOTS * SLOTS,), jnp.int32),
            pltpu.VMEM((SLOTS * block, SLOTS * block), jnp.bfloat16),
            pltpu.VMEM((SLOTS * block, SLOTS * block), jnp.bfloat16),
            pltpu.SemaphoreType.DMA((22 * CHUNKS,)),
            pltpu.SemaphoreType.DMA((22 * CHUNKS,)),
            pltpu.SemaphoreType.DMA((8,)),
            pltpu.SemaphoreType.DMA((8,)),
            pltpu.SemaphoreType.DMA((3,)),
        ],
        compiler_params=pltpu.CompilerParams(
            collective_id=0, has_side_effects=True, vmem_limit_bytes=32 * 1024 * 1024
        ),
    )(
        pattern.reshape((SITES, SLOTS)),
        retained.reshape((SITES, SLOTS)),
        density.reshape((SITES * SLOTS, block, block)),
    )
    return out.reshape(density.shape)


def solution(mesh):
    rows, cols = mesh.shape["row"], mesh.shape["col"]
    return jax.shard_map(
        lambda *args: on_device(rows, cols, *args),
        mesh=mesh,
        in_specs=(P("row", "col", None, None, None), P("row", "col", None), P("row", "col", None)),
        out_specs=P("row", "col", None, None, None),
        check_vma=False,
    )
```

time: 54.4 us -> 48.8 us (0.90)
  the two profiles are of different devices: /device:TPU:0 before, /device:TPU:1 now
where the time goes in v2:
time: 48.8 us; the launch traced here: 48 us
  Pallas kernels  45.5 us (93%)
  local copies, waits for them, and re-layouts  2.53 us (5%)
    pallas_call x1, Pallas kernels, on_device(): pl.pallas_call(lambda *refs: kernel(rows, cols, *refs), out_shape=jax.Sha...  45.5 us
    unnamed x7, local copies, waits for them, and re-layouts  2.53 us

profile of v2, /device:TPU:1, one launch (start us, length us, event | category | flops | bytes accessed | tf_op | source)
XLA Modules:
  0.0 48.0 jit_solution(16338388856162408000)
XLA Ops:
  0.0 0.0 copy-start.2
  0.0 0.0 copy-start.1
  0.0 0.7 %copy-done.2 = s32[1,2,4]{2,1,0:T(2,128)S(1)} copy-done((s32[1,2,4]{2,1,0:T(2,128)S(1)}, s32[1,2,4]{2,1,0:T(2,128)}, u32[]{:S(2)}) %copy-start.2) | copy-done | bytes 56
  0.7 0.0 copy-done.1
  0.7 0.0 copy-start
  0.7 1.0 %copy-done = f32[1,2,4,128,128]{4,3,2,1,0:T(8,128)S(1)} copy-done((f32[1,2,4,128,128]{4,3,2,1,0:T(8,128)S(1)}, f32[1,2,4,128,128]{4,3,2,1,0:T(8,128)}, u32[]{:S(2)}) %copy-start) | copy-done | bytes 524312
  1.7 45.5 %shard_map.37 = f32[8,128,128]{2,1,0:T(8,128)S(1)} custom-call(s32[2,4]{1,0:T(2,128)S(1)} %bitcast.6, s32[2,4]{1,0:T(2,128)S(1)} %bitcast.7, f32[8,128,128]{2,1,0:T(8,128)S(1)} %bitcast.5), custom_call_target="tpu_custom_call" | custom-call | tf_op jit(solution)/shard_map/pallas_call | solution.py:296
  47.2 0.8 %copy.5 = f32[1,2,4,128,128]{4,3,2,1,0:T(8,128)} copy(f32[1,2,4,128,128]{4,3,2,1,0:T(8,128)S(1)} %bitcast.4) | data formatting | bytes 1048576
Async XLA Ops:
  0.0 0.7 %copy-start.2 = (s32[1,2,4]{2,1,0:T(2,128)S(1)}, s32[1,2,4]{2,1,0:T(2,128)}, u32[]{:S(2)}) copy-start(s32[1,2,4]{2,1,0:T(2,128)} %param.5) | copy-start | bytes 100
  0.0 0.7 %copy-start.1 = (s32[1,2,4]{2,1,0:T(2,128)S(1)}, s32[1,2,4]{2,1,0:T(2,128)}, u32[]{:S(2)}) copy-start(s32[1,2,4]{2,1,0:T(2,128)} %param.4) | copy-start | bytes 100
  0.7 1.0 %copy-start = (f32[1,2,4,128,128]{4,3,2,1,0:T(8,128)S(1)}, f32[1,2,4,128,128]{4,3,2,1,0:T(8,128)}, u32[]{:S(2)}) copy-start(f32[1,2,4,128,128]{4,3,2,1,0:T(8,128)} %param.3) | copy-start | bytes 1572868

commit v3 on v2

--- a/solution.py
+++ b/solution.py
@@ -22,7 +22,7 @@
 
 def kernel(
     rows, cols, pattern_ref, retained_ref, density_ref, out_ref,
-    near0, near1, held, packed, codes, scalars, table, right_high, right_low,
+    near0, near1, far0, far1, own_codes, held, packed, codes, scalars, table, right_high, right_low,
     send_sem, recv_sem, code_send, code_recv, local_sem,
 ):
     block = out_ref.shape[-1]
@@ -47,10 +47,19 @@
     )
     load_held.start()
     held[SITES * SLOTS] = jnp.zeros((block, block), jnp.float32)
+    load_codes = [
+        pltpu.make_async_copy(ref, own_codes.at[k], local_sem.at[3 + k])
+        for k, ref in enumerate((pattern_ref, retained_ref))
+    ]
+    for copy in load_codes:
+        copy.start()
     for j in range(SITES):
         codes[own + j] = jnp.zeros(codes.shape[1:], jnp.int32)
-        for k, ref in enumerate((pattern_ref, retained_ref)):
-            code = ref[j:j + 1, :]
+    for copy in load_codes:
+        copy.wait()
+    for j in range(SITES):
+        for k in range(2):
+            code = own_codes[k, j:j + 1, :]
             third = jnp.where(code >= 6, 2, jnp.where(code >= 3, 1, 0))
             codes[own + j, k:k + 1, 0:SLOTS] = code + 2 * third - 6
             codes[own + j, 2 + k:3 + k, 0:SLOTS] = code + third - 5
@@ -80,38 +89,47 @@
     def code_copy(index, source, target, size, device):
         return send(codes, codes, source, target, size, (code_send, code_recv), index, device)
 
-    def block_copy(step, kind, chunk, part, source, target, device, from_ref=None, start=None):
-        near = (near0, near1)[step]
+    def block_copy(step, kind, chunk, part, source, target, device, from_ref, to_ref, start=None):
         index = (step * 11 + kind) * CHUNKS + chunk
         first = source * SLOTS + chunk * part if start is None else start
         return send(
-            near if from_ref is None else from_ref, near, first, target * SLOTS + chunk * part,
+            from_ref, to_ref, first, target * SLOTS + chunk * part,
             part, (send_sem, recv_sem), index, device,
         )
 
     parts = (2 // CHUNKS, SLOTS // CHUNKS)
+    nears, fars = (near0, near1), (far0, far1)
 
     def to_pair(step, role, chunk):
         column, part = here[role], parts[step]
         target = handed * WIDE + column
         if step == 0:
             start = (column - 1) * 2 + chunk * part
-            return block_copy(0, role, chunk, part, 0, target, (pair, col), packed, start)
-        return block_copy(1, role, chunk, part, WIDE + column, target, (pair, col))
+            return block_copy(0, role, chunk, part, 0, target, (pair, col), packed, near0, start)
+        return block_copy(
+            1, role, chunk, part, WIDE + column, target, (pair, col), near1, near1
+        )
 
     def hand_on(step, role, chunk):
-        column = (here + (outer_in,))[role]
+        near, far = nears[step], fars[step]
+        if role == 2:
+            return block_copy(
+                step, 4, chunk, parts[step], paired, handed, (onward, col), far, far
+            )
+        column = here[role]
         return block_copy(
             step, 2 + role, chunk, parts[step],
-            paired * WIDE + column, handed * WIDE + column, (onward, col),
+            paired * WIDE + column, handed * WIDE + column, (onward, col), near, near,
         )
 
     def sideways(step, place, role, chunk):
         part = SLOTS // CHUNKS if place == 0 else parts[step]
+        near, far = nears[step], fars[step]
         base = window_rows[place] * WIDE
+        target = base + there[1] if role else window_rows[place]
         return block_copy(
             step, 5 + 2 * place + role, chunk, part,
-            base + here[role], base + there[role], (row, beside[role]),
+            base + here[role], target, (row, beside[role]), near, near if role else far,
         )
 
     def begin(step, role):
@@ -121,30 +139,45 @@
             sideways(step, 0, role, chunk).start()
 
     def relay(step):
-        for role in range(2):
+        for role in ((0, 1), (1, 0))[step]:
             for chunk in range(CHUNKS):
                 to_pair(step, role, chunk).wait_recv()
                 hand_on(step, role, chunk).start()
                 sideways(step, 1, role, chunk).start()
+
+        def inner():
+            for chunk in range(CHUNKS):
+                hand_on(step, 1, chunk).wait_recv()
+                sideways(step, 2, 1, chunk).start()
+
+        if step == 1:
+            inner()
         hand_on(step, 0, 0).wait_recv()
         sideways(step, 2, 0, 0).start()
         sideways(step, 1, 0, 1).wait_recv()
         hand_on(step, 2, 1).start()
         hand_on(step, 0, 1).wait_recv()
-        for chunk in range(CHUNKS):
-            hand_on(step, 1, chunk).wait_recv()
-            sideways(step, 2, 1, chunk).start()
-
-    def finish(step):
-        for chunk in range(CHUNKS):
-            for role in range(2):
-                sideways(step, 0, role, chunk).wait_recv()
+        if step == 0:
+            inner()
+
+    def inner_arrives(step):
+        for chunk in range(CHUNKS):
+            for place in range(3):
+                sideways(step, place, 1, chunk).wait_recv()
+
+    def outer_arrives(step):
+        for chunk in range(CHUNKS):
+            sideways(step, 0, 0, chunk).wait_recv()
         sideways(step, 1, 0, 0).wait_recv()
         sideways(step, 2, 0, 0).wait_recv()
         hand_on(step, 2, 1).wait_recv()
-        for chunk in range(CHUNKS):
-            for place in (1, 2):
-                sideways(step, place, 1, chunk).wait_recv()
+        near, far = nears[step], fars[step]
+        for window_row in range(3):
+            count = SLOTS if step == 1 or window_row == 1 else 2
+            for t in range(count):
+                near[(window_row * WIDE + outer_in) * SLOTS + t] = far[window_row * SLOTS + t]
+
+    def all_sent(step):
         for chunk in range(CHUNKS):
             for role in range(2):
                 to_pair(step, role, chunk).wait_send()
@@ -241,13 +274,13 @@
 
     fill(0, 0, 0, True)
     fill(1, 1, 0, True)
-    fill(2, 1, 1, False)
-    finish(0)
-    for column in (0, WIDE - 1):
+
+    def flip_side(column):
         for t in range(1, SLOTS):
             flip((WIDE + column) * SLOTS + t, FLIPPED + column * SLOTS + t)
-    for k in range(2):
-        for column in range(WIDE - 1):
+
+    def flip_edge(column):
+        for k in range(2):
             flip((2 * k * WIDE + column) * SLOTS + 1, FLIPPED + (SLOTS + k) * WIDE + column)
 
     def gather(near, number, j):
@@ -276,18 +309,36 @@
             gather(near, numbers[1], j)
         return 3.0 * square - 2.0 * product(square)
 
-    for role in range(2):
+    def first_step(role):
         j = here[role] - 1
         result = purify(near0, (0, 1), j)
         for u in range(SLOTS):
             near1[(own + j) * SLOTS + u] = result[:, u * block:(u + 1) * block]
         begin(1, role)
-    relay(1)
-    finish(1)
-    for j in range(SITES):
+
+    def second_step(role):
+        j = here[role] - 1
         result = purify(near1, (2, 2), j)
         for u in range(SLOTS):
             out_ref[j * SLOTS + u] = result[:, u * block:(u + 1) * block]
+
+    inner_arrives(0)
+    flip_side(WIDE - 1 - outer_in)
+    flip_edge(1)
+    flip_edge(2 - 2 * core)
+    first_step(1)
+    outer_arrives(0)
+    flip_side(outer_in)
+    flip_edge(2 * core)
+    first_step(0)
+    relay(1)
+    fill(2, 1, 1, False)
+    inner_arrives(1)
+    second_step(1)
+    outer_arrives(1)
+    second_step(0)
+    all_sent(0)
+    all_sent(1)
 
 
 def on_device(rows, cols, density, pattern, retained):
@@ -296,11 +347,14 @@
     out = pl.pallas_call(
         lambda *refs: kernel(rows, cols, *refs),
         out_shape=jax.ShapeDtypeStruct((SITES * SLOTS, block, block), jnp.float32),
-        in_specs=[vmem, vmem, pl.BlockSpec(memory_space=pl.ANY)],
+        in_specs=[pl.BlockSpec(memory_space=pltpu.HBM)] * 3,
         out_specs=vmem,
         scratch_shapes=[
             pltpu.VMEM((FLIPPED + WIDE * SLOTS + 2 * WIDE, block, block), jnp.float32),
             pltpu.VMEM((ZERO_BLOCK + 1, block, block), jnp.float32),
+            pltpu.VMEM((3 * SLOTS, block, block), jnp.float32),
+            pltpu.VMEM((3 * SLOTS, block, block), jnp.float32),
+            pltpu.VMEM((2, SITES, SLOTS), jnp.int32),
             pltpu.VMEM((SITES * SLOTS + 1, block, block), jnp.float32),
             pltpu.VMEM((2 * SITES, block, block), jnp.float32),
             pltpu.VMEM((3 * WIDE, 8, 128), jnp.int32),
@@ -312,7 +366,7 @@
             pltpu.SemaphoreType.DMA((22 * CHUNKS,)),
             pltpu.SemaphoreType.DMA((8,)),
             pltpu.SemaphoreType.DMA((8,)),
-            pltpu.SemaphoreType.DMA((3,)),
+            pltpu.SemaphoreType.DMA((5,)),
         ],
         compiler_params=pltpu.CompilerParams(
             collective_id=0, has_side_effects=True, vmem_limit_bytes=32 * 1024 * 1024

time: 48.8 us -> 48 us (0.984); the launches traced: 48 us -> 47.8 us
  no operation moved by 1% of the time
where the time goes in v3:
time: 48 us; the launch traced here: 47.8 us
  Pallas kernels  45.3 us (94%)
  local copies, waits for them, and re-layouts  2.53 us (5%)
    pallas_call x1, Pallas kernels, on_device(): pl.pallas_call(lambda *refs: kernel(rows, cols, *refs), out_shape=jax.Sha...  45.3 us
    unnamed x7, local copies, waits for them, and re-layouts  2.53 us

profile of v3, /device:TPU:1, one launch (start us, length us, event | category | flops | bytes accessed | tf_op | source)
XLA Modules:
  0.0 47.8 jit_solution(9659703208007073571)
XLA Ops:
  0.0 0.0 copy-start.2
  0.0 0.0 copy-start.1
  0.0 0.7 %copy-done.2 = s32[1,2,4]{2,1,0:T(2,128)S(1)} copy-done((s32[1,2,4]{2,1,0:T(2,128)S(1)}, s32[1,2,4]{2,1,0:T(2,128)}, u32[]{:S(2)}) %copy-start.2) | copy-done | bytes 56
  0.7 0.0 copy-done.1
  0.7 0.0 copy-start
  0.7 1.0 %copy-done = f32[1,2,4,128,128]{4,3,2,1,0:T(8,128)S(1)} copy-done((f32[1,2,4,128,128]{4,3,2,1,0:T(8,128)S(1)}, f32[1,2,4,128,128]{4,3,2,1,0:T(8,128)}, u32[]{:S(2)}) %copy-start) | copy-done | bytes 524312
  1.7 45.3 %shard_map.37 = f32[8,128,128]{2,1,0:T(8,128)S(1)} custom-call(s32[2,4]{1,0:T(2,128)S(1)} %bitcast.6, s32[2,4]{1,0:T(2,128)S(1)} %bitcast.7, f32[8,128,128]{2,1,0:T(8,128)S(1)} %bitcast.5), custom_call_target="tpu_custom_call" | custom-call | tf_op jit(solution)/shard_map/pallas_call | solution.py:347
  47.1 0.8 %copy.5 = f32[1,2,4,128,128]{4,3,2,1,0:T(8,128)} copy(f32[1,2,4,128,128]{4,3,2,1,0:T(8,128)S(1)} %bitcast.4) | data formatting | bytes 1048576
Async XLA Ops:
  0.0 0.7 %copy-start.2 = (s32[1,2,4]{2,1,0:T(2,128)S(1)}, s32[1,2,4]{2,1,0:T(2,128)}, u32[]{:S(2)}) copy-start(s32[1,2,4]{2,1,0:T(2,128)} %param.5) | copy-start | bytes 100
  0.0 0.7 %copy-start.1 = (s32[1,2,4]{2,1,0:T(2,128)S(1)}, s32[1,2,4]{2,1,0:T(2,128)}, u32[]{:S(2)}) copy-start(s32[1,2,4]{2,1,0:T(2,128)} %param.4) | copy-start | bytes 100
  0.7 1.0 %copy-start = (f32[1,2,4,128,128]{4,3,2,1,0:T(8,128)S(1)}, f32[1,2,4,128,128]{4,3,2,1,0:T(8,128)}, u32[]{:S(2)}) copy-start(f32[1,2,4,128,128]{4,3,2,1,0:T(8,128)} %param.3) | copy-start | bytes 1572868

commit v4 on v3

--- a/solution.py
+++ b/solution.py
@@ -369,7 +369,7 @@
             pltpu.SemaphoreType.DMA((5,)),
         ],
         compiler_params=pltpu.CompilerParams(
-            collective_id=0, has_side_effects=True, vmem_limit_bytes=32 * 1024 * 1024
+            collective_id=0, has_side_effects=True, vmem_limit_bytes=63 * 1024 * 1024
         ),
     )(
         pattern.reshape((SITES, SLOTS)),

time: 48 us -> 49.1 us (1.023)
  Pallas kernels: 45.3 us -> 47.1 us
  local copies, waits for them, and re-layouts: 2.53 us -> 1.87 us
    pallas_call x1, Pallas kernels: 45.3 us -> 47.1 us  [on_device(): pl.pallas_call(lambda *refs: kernel(rows, cols, *refs), out_shape=jax.Sha...]
    unnamed x7 -> x1, local copies, waits for them, and re-layouts: 2.53 us -> 1.87 us
where the time goes in v4:
time: 49.1 us; the launch traced here: 49 us
  Pallas kernels  47.1 us (96%)
  local copies, waits for them, and re-layouts  1.87 us (4%)
    pallas_call x1, Pallas kernels, on_device(): pl.pallas_call(lambda *refs: kernel(rows, cols, *refs), out_shape=jax.Sha...  47.1 us
    unnamed x1, local copies, waits for them, and re-layouts  1.87 us

profile of v4, /device:TPU:1, one launch (start us, length us, event | category | flops | bytes accessed | tf_op | source)
XLA Modules:
  0.0 49.0 jit_solution(733948758975694252)
XLA Ops:
  0.0 47.1 %shard_map.37 = f32[8,128,128]{2,1,0:T(8,128)} custom-call(s32[2,4]{1,0:T(2,128)} %bitcast.6, s32[2,4]{1,0:T(2,128)} %bitcast.7, f32[8,128,128]{2,1,0:T(8,128)} %bitcast.5), custom_call_target="tpu_custom_call" | custom-call | tf_op jit(solution)/shard_map/pallas_call | solution.py:347
  47.1 1.9 %copy.5 = f32[1,2,4,128,128]{4,3,2,1,0:T(8,128)} copy(f32[1,2,4,128,128]{4,3,2,1,0:T(8,128)} %bitcast.4) | data formatting | bytes 1048576

commit v5 on v3

--- a/solution.py
+++ b/solution.py
@@ -132,11 +132,13 @@
             base + here[role], target, (row, beside[role]), near, near if role else far,
         )
 
-    def begin(step, role):
+    def begin_row(step, role):
+        for chunk in range(CHUNKS):
+            sideways(step, 0, role, chunk).start()
+
+    def begin_pair(step, role):
         for chunk in range(CHUNKS):
             to_pair(step, role, chunk).start()
-        for chunk in range(CHUNKS):
-            sideways(step, 0, role, chunk).start()
 
     def relay(step):
         for role in ((0, 1), (1, 0))[step]:
@@ -205,17 +207,19 @@
     codes_pair.start()
     for copy in codes_side[0]:
         copy.start()
+    load.wait()
+    begin_row(0, 0)
+    load_held.wait()
     own_scalars.wait()
-    load_held.wait()
     for j in range(SITES):
         packed[2 * j] = held[j * SLOTS]
         found = jnp.int32(SITES * SLOTS)
         for t in range(1, SLOTS):
             found = jnp.where(scalars[own + j, 0, t] == 1, j * SLOTS + t, found)
         packed[2 * j + 1] = held[found]
-    load.wait()
     for role in range(2):
-        begin(0, role)
+        begin_pair(0, role)
+    begin_row(0, 1)
     for j in range(SITES):
         for t in range(1, SLOTS):
             flip((own + j) * SLOTS + t, FLIPPED + (1 + j) * SLOTS + t)
@@ -283,8 +287,8 @@
         for k in range(2):
             flip((2 * k * WIDE + column) * SLOTS + 1, FLIPPED + (SLOTS + k) * WIDE + column)
 
-    def gather(near, number, j):
-        for s in range(SLOTS):
+    def gather(near, number, j, start=0):
+        for s in range(start, SLOTS):
             for u in range(SLOTS):
                 found = table[((number * SITES + j) * SLOTS + s) * SLOTS + u]
                 high, low = split(near[found])
@@ -306,7 +310,7 @@
         )
         square = product(mine)
         if numbers[1] != numbers[0]:
-            gather(near, numbers[1], j)
+            gather(near, numbers[1], j, 1)
         return 3.0 * square - 2.0 * product(square)
 
     def first_step(role):
@@ -314,7 +318,8 @@
         result = purify(near0, (0, 1), j)
         for u in range(SLOTS):
             near1[(own + j) * SLOTS + u] = result[:, u * block:(u + 1) * block]
-        begin(1, role)
+        begin_row(1, role)
+        begin_pair(1, role)
 
     def second_step(role):
         j = here[role] - 1

time: 48 us -> 48 us (level)
  no operation moved by 1% of the time
where the time goes in v5:
time: 48 us; the launch traced here: 47.8 us
  Pallas kernels  45.3 us (94%)
  local copies, waits for them, and re-layouts  2.53 us (5%)
    pallas_call x1, Pallas kernels, on_device(): pl.pallas_call(lambda *refs: kernel(rows, cols, *refs), out_shape=jax.Sha...  45.3 us
    unnamed x7, local copies, waits for them, and re-layouts  2.53 us

profile of v5, /device:TPU:1, one launch (start us, length us, event | category | flops | bytes accessed | tf_op | source)
XLA Modules:
  0.0 47.8 jit_solution(15168621886659952794)
XLA Ops:
  0.0 0.0 copy-start.2
  0.0 0.0 copy-start.1
  0.0 0.7 %copy-done.2 = s32[1,2,4]{2,1,0:T(2,128)S(1)} copy-done((s32[1,2,4]{2,1,0:T(2,128)S(1)}, s32[1,2,4]{2,1,0:T(2,128)}, u32[]{:S(2)}) %copy-start.2) | copy-done | bytes 56
  0.7 0.0 copy-done.1
  0.7 0.0 copy-start
  0.7 1.0 %copy-done = f32[1,2,4,128,128]{4,3,2,1,0:T(8,128)S(1)} copy-done((f32[1,2,4,128,128]{4,3,2,1,0:T(8,128)S(1)}, f32[1,2,4,128,128]{4,3,2,1,0:T(8,128)}, u32[]{:S(2)}) %copy-start) | copy-done | bytes 524312
  1.7 45.3 %shard_map.37 = f32[8,128,128]{2,1,0:T(8,128)S(1)} custom-call(s32[2,4]{1,0:T(2,128)S(1)} %bitcast.6, s32[2,4]{1,0:T(2,128)S(1)} %bitcast.7, f32[8,128,128]{2,1,0:T(8,128)S(1)} %bitcast.5), custom_call_target="tpu_custom_call" | custom-call | tf_op jit(solution)/shard_map/pallas_call | solution.py:352
  47.0 0.8 %copy.5 = f32[1,2,4,128,128]{4,3,2,1,0:T(8,128)} copy(f32[1,2,4,128,128]{4,3,2,1,0:T(8,128)S(1)} %bitcast.4) | data formatting | bytes 1048576
Async XLA Ops:
  0.0 0.7 %copy-start.2 = (s32[1,2,4]{2,1,0:T(2,128)S(1)}, s32[1,2,4]{2,1,0:T(2,128)}, u32[]{:S(2)}) copy-start(s32[1,2,4]{2,1,0:T(2,128)} %param.5) | copy-start | bytes 100
  0.0 0.7 %copy-start.1 = (s32[1,2,4]{2,1,0:T(2,128)S(1)}, s32[1,2,4]{2,1,0:T(2,128)}, u32[]{:S(2)}) copy-start(s32[1,2,4]{2,1,0:T(2,128)} %param.4) | copy-start | bytes 100
  0.7 1.0 %copy-start = (f32[1,2,4,128,128]{4,3,2,1,0:T(8,128)S(1)}, f32[1,2,4,128,128]{4,3,2,1,0:T(8,128)}, u32[]{:S(2)}) copy-start(f32[1,2,4,128,128]{4,3,2,1,0:T(8,128)} %param.3) | copy-start | bytes 1572868
